TPU v7x, 32 devices: a whole 2x2x4 slice. The times are simulated.
32 devices in a mesh: parts: 2 (over y), rows: 4 (over z), cols: 2 (over x), layers: 2 (over core).
Axes of the slice: x: 2, y: 2, z: 4, core: 2. Of those that a mesh axis runs over, the one named last changes fastest.
Arguments:
- a_blocks: float32 [8, 2, 2, 32, 128, 128], P(('parts', 'rows'), 'cols', 'layers'), parts along dimension 0, may hold values from -6 to 6
- a_rows: int32 [8, 2, 2, 32], P(('parts', 'rows'), 'cols', 'layers'), parts along dimension 0, may hold values from 0 to 7
- b_blocks: float32 [8, 2, 2, 8, 128, 128], P(('parts', 'rows'), 'cols', 'layers'), parts along dimension 0, may hold values from -0.5 to 0.5
- b_cols: int32 [8, 2, 2, 8], P(('parts', 'rows'), 'cols', 'layers'), parts along dimension 0, may hold values from 0 to 7
- pairs: int32 [8, 2, 2, 2, 2, 96], P(('parts', 'rows'), 'cols', 'layers'), parts along dimension 0, may hold values from 0 to 31, as said below
- counts: int32 [8, 2, 2, 2], P(('parts', 'rows'), 'cols', 'layers'), parts along dimension 0, may hold values from 1 to 96, as said below
- kept: int32 [8, 2, 8, 8], P(('parts', 'rows'), 'cols'), parts along dimension 0, may hold values from -1 to 47, as said below
Outputs:
- c_blocks: float32 [8, 2, 48, 128, 128], P(('parts', 'rows'), 'cols', 'layers'), parts along dimension 0
There are 2 independent parts, one for each index of `parts`. A program takes and returns all parts, laid end to end along the dimension named above; each array names one. Nothing has to cross between parts.
Inputs may be any that keep to these rules, and one draw needn't show every extreme that they name: In each list the pairs are distinct and meet in shared inner block indices of the two panels; the first entry indexes the 32 A blocks, the second the 8 B blocks. `counts`: some list is full in every draw. `kept`: in each tile every slot 0 to 47 stands exactly once; all other entries are -1.
All inputs are finite; a program needn't handle non-finite values.
Results may differ from a plain program's by a relative error of at most 0.0003.
Values sent between devices are 32-bit elements; how exact they have to be, the bound alone decides.
A program may use at most 64 MiB of HBM per device.

v0:
```python
import functools

import jax
import jax.numpy as jnp
from jax import lax
from jax.experimental import pallas as pl
from jax.experimental.pallas import tpu as pltpu
from jax.sharding import PartitionSpec as P

TILE_COLS = 8
KEPT = 48
A_BLOCKS = 32
B_BLOCKS = 8
CHUNKS = (25, 7)
UNROLL = 4


def from_behind(value, axis, by=1):
    peers = lax.axis_size(axis)
    return lax.ppermute(value, axis, [(i, (i + by) % peers) for i in range(peers)])


def split(block):
    high = block.astype(jnp.bfloat16)
    low = (block - high.astype(jnp.float32)).astype(jnp.bfloat16)
    return high, low


def product(left, right):
    left_high, left_low = split(left)
    right_high, right_low = split(right)
    lefts = jnp.concatenate([left_high, left_low], axis=1)
    rights = jnp.concatenate([right_high, right_low], axis=1)
    rights = jnp.concatenate([rights, rights], axis=0)
    both = jnp.dot(lefts, rights, preferred_element_type=jnp.float32)
    return both[:, : left.shape[1]] + both[:, left.shape[1] :]


def find(bounds, slots, own, other, kept, lists):
    base = lax.axis_index("layers") * slots
    chunk_count = len(bounds) - 1
    for row in range(2 * (chunk_count + 1)):
        lists[row, 0] = 0
    for side, table in enumerate((own, other)):
        pairs_at = 1 + A_BLOCKS + B_BLOCKS
        pair_count = (table.shape[0] - pairs_at) // 2

        def scan(q, carry):
            i = table[pairs_at + q]
            j = table[pairs_at + pair_count + q]
            slot = kept[table[1 + i] * TILE_COLS + table[1 + A_BLOCKS + j]] - base
            chunk = jnp.int32(0)
            first = jnp.int32(0)
            for low, high in zip(bounds[1:-1], bounds[1:-1]):
                chunk = chunk + (i >= low).astype(jnp.int32)
                first = jnp.where(i >= low, high, first)
            use = (slot >= 0) & (slot < slots)
            row = 2 * jnp.where(use, chunk, chunk_count) + side
            place = lists[row, 0] + 1
            lists[row, 0] = place
            lists[row, place] = (i - first) + 64 * j + 1024 * jnp.where(use, slot, slots)
            return carry

        lax.fori_loop(0, table[0], scan, 0)
    for row in range(2 * chunk_count):
        end = lists[row, 0] + 1
        for extra in range(UNROLL):
            lists[row, end + extra] = 1024 * slots


def find_pairs(bounds, tables, kept):
    slots = KEPT // lax.axis_size("layers")
    smem = pl.BlockSpec(memory_space=pltpu.SMEM)
    rows = 2 * len(bounds)
    return pl.pallas_call(
        functools.partial(find, bounds, slots),
        out_shape=jax.ShapeDtypeStruct((rows, 128), jnp.int32),
        in_specs=[smem] * 3,
        out_specs=smem,
        cost_estimate=pl.CostEstimate(flops=10**6, bytes_accessed=1 << 20, transcendentals=0),
    )(*tables, kept)


def add_products(chunk, lists, *refs):
    panels, (seed, out, total) = refs[:4], refs[4:]
    slots, width = out.shape[0], out.shape[1]
    if seed is None:
        total[...] = jnp.zeros_like(total)
    else:
        total[:slots] = seed[...]
        total[slots] = jnp.zeros((width, width), jnp.float32)
    for side in range(2):
        a_ref, b_ref = panels[side], panels[2 + side]
        row = 2 * chunk + side

        def step(turn, carry):
            codes = [lists[row, 1 + turn * UNROLL + u] for u in range(UNROLL)]
            values = [product(a_ref[code & 63], b_ref[(code >> 6) & 15]) for code in codes]
            for code, value in zip(codes, values):
                total[code >> 10] += value
            return carry

        lax.fori_loop(0, (lists[row, 0] + UNROLL - 1) // UNROLL, step, 0)
    out[...] = total[:slots]


def accumulate(chunk, lists, a_panels, b_panels, seed):
    width = a_panels[0].shape[-1]
    slots = KEPT // lax.axis_size("layers")
    smem, vmem = pl.BlockSpec(memory_space=pltpu.SMEM), pl.BlockSpec(memory_space=pltpu.VMEM)
    operands = [lists, *a_panels, *b_panels] + ([] if seed is None else [seed])

    def body(*refs):
        if seed is None:
            refs = refs[:5] + (None,) + refs[5:]
        add_products(chunk, *refs)

    return pl.pallas_call(
        body,
        out_shape=jax.ShapeDtypeStruct((slots, width, width), jnp.float32),
        in_specs=[smem] + [vmem] * (len(operands) - 1),
        out_specs=vmem,
        scratch_shapes=[pltpu.VMEM((slots + 1, width, width), jnp.float32)],
        compiler_params=pltpu.CompilerParams(vmem_limit_bytes=32 << 20),
        cost_estimate=pl.CostEstimate(flops=10**9, bytes_accessed=6 << 20, transcendentals=0),
    )(*operands)


def on_device(a_blocks, a_rows, b_blocks, b_cols, pairs, counts, kept):
    a_own, b_own = a_blocks[0, 0, 0], b_blocks[0, 0, 0]
    rows_own, cols_own = a_rows[0, 0, 0], b_cols[0, 0, 0]
    pair_table, live = pairs[0, 0, 0], counts[0, 0, 0]
    slot_table = kept[0, 0].reshape(-1)

    def table(step, rows, cols):
        return jnp.concatenate([live[step : step + 1], rows, cols, pair_table[step].reshape(-1)])

    def with_other(value):
        return value, from_behind(value, "layers")

    rows_next = from_behind(rows_own, "rows")
    bounds = (0,)
    for size in CHUNKS:
        bounds += (bounds[-1] + size,)
    pieces = [a_own[s:e] for s, e in zip(bounds, bounds[1:])]
    pieces[0], rows_next = lax.optimization_barrier((pieces[0], rows_next))
    chunks = [from_behind(pieces[0], "rows")]
    b_next = from_behind(b_own, "cols")
    cols_next = from_behind(cols_own, "cols")
    tables = with_other(table(0, rows_own, cols_own))
    lists = find_pairs((0, A_BLOCKS), tables, slot_table)
    sums = accumulate(0, lists, with_other(a_own), with_other(b_own), None)
    rows_next, cols_next, b_next, sums = lax.optimization_barrier(
        (rows_next, cols_next, b_next, sums)
    )
    b_next = with_other(b_next)
    tables = with_other(table(1, rows_next, cols_next))
    lists = find_pairs(bounds, tables, slot_table)
    chunk, piece, lists, sums = lax.optimization_barrier((chunks[0], pieces[1], lists, sums))
    last = from_behind(piece, "rows")
    sums = accumulate(0, lists, with_other(chunk), b_next, sums)
    last, sums = lax.optimization_barrier((last, sums))
    sums = accumulate(1, lists, with_other(last), b_next, sums)
    return sums[None, None]


def solution(mesh):
    return jax.shard_map(
        on_device,
        mesh=mesh,
        in_specs=(
            P(("parts", "rows"), "cols", "layers", None, None, None),
            P(("parts", "rows"), "cols", "layers", None),
            P(("parts", "rows"), "cols", "layers", None, None, None),
            P(("parts", "rows"), "cols", "layers", None),
            P(("parts", "rows"), "cols", "layers", None, None, None),
            P(("parts", "rows"), "cols", "layers", None),
            P(("parts", "rows"), "cols", None, None),
        ),
        out_specs=P(("parts", "rows"), "cols", "layers", None, None),
        check_vma=False,
    )
```

profile of v0, /device:TPU:0, one launch (start us, length us, event | category | flops | bytes accessed | tf_op | source)
XLA Modules:
  0.0 65.3 jit_solution(16510910647139543863)
XLA Ops:
  0.5 2.6 %collective-permute-start = (s32[32]{0:T(128)}, s32[32]{0:T(128)S(1)}, u32[]{:S(2)}, u32[]{:S(2)}) collective-permute-start(s32[32]{0:T(128)} %bitcast.18), channel_id=1, source_target_pairs={{0,4},{4,8},{8,12},{12,0},{1,5},{5,9},{9,13},{13,1},{2,6},{6,10},{... | collective-permute-start | bytes 392 | tf_op jit(solution)/shard_map/ppermute | solution.py:20
  3.1 2.8 %slice_bitcast_fusion = f32[25,128,128]{2,1,0:T(8,128)} fusion(f32[1,1,1,32,128,128]{5,4,3,2,1,0:T(8,128)} %param.7), kind=kLoop, calls=%fused_computation | loop fusion | bytes 3276800 | tf_op jit(solution)/shard_map/slice | solution.py:145
  5.9 0.9 %collective-permute-done = s32[32]{0:T(128)S(1)} collective-permute-done((s32[32]{0:T(128)}, s32[32]{0:T(128)S(1)}, u32[]{:S(2)}, u32[]{:S(2)}) %collective-permute-start) | collective-permute-done | bytes 160 | tf_op jit(solution)/shard_map/ppermute | solution.py:20
  6.8 0.7 %collective-permute-start.1 = (f32[25,128,128]{2,1,0:T(8,128)}, f32[25,128,128]{2,1,0:T(8,128)}, u32[]{:S(2)}, u32[]{:S(2)}) collective-permute-start(f32[25,128,128]{2,1,0:T(8,128)} %slice_bitcast_fusion), channel_id=1, source_target_pairs={{0,4},{4,8},{8,12},{12,0},{1,5},{5,9},{9,13},{13,1},{2,6},{6,10},{... | collective-permute-start | bytes 4915208 | tf_op jit(solution)/shard_map/ppermute | solution.py:20
  7.5 1.5 %collective-permute-start.3 = (f32[8,128,128]{2,1,0:T(8,128)S(1)}, f32[8,128,128]{2,1,0:T(8,128)S(1)}, u32[]{:S(2)}, u32[]{:S(2)}) collective-permute-start(f32[8,128,128]{2,1,0:T(8,128)S(1)} %bitcast.16), channel_id=1, source_target_pairs={{0,2},{2,0},{1,3},{3,1},{4,6},{6,4},{5,7},{7,5},{8,10},{10,8},{9,1... | collective-permute-start | bytes 1572872 | tf_op jit(solution)/shard_map/ppermute | solution.py:20
  9.1 0.6 fusion.1
  9.7 0.7 %pad_add_fusion.own = s32[233]{0:T(256)S(1)} fusion(s32[192]{0:T(256)S(1)} %reshape_squeeze.9, s32[8]{0:T(128)S(1)} %bitcast.20, s32[32]{0:T(128)S(1)} %bitcast.19, s32[1]{0:T(128)} %bitcast.6), kind=kLoop, calls=%fused_computation.2 | loop fusion | flops 699 | bytes 1864 | tf_op jit(solution)/shard_map/concatenate | solution.py:136
  10.6 0.6 reshape_squeeze.10.kept
  12.1 3.6 %shard_map.73.refs_0_ = s32[4,128]{1,0:T(4,128)} custom-call(s32[233]{0:T(256)} %copy-done.7, s32[233]{0:T(256)} %copy-done.11, s32[64]{0:T(128)} %reshape_squeeze.10.kept), custom_call_target="tpu_custom_call" | custom-call | flops 1000000 | bytes 1048576 | tf_op jit(solution)/shard_map/pallas_call | solution.py:75
  15.7 0.7 %copy-done.5 = s32[4,128]{1,0:T(4,128)S(1)} copy-done((s32[4,128]{1,0:T(4,128)S(1)}, s32[4,128]{1,0:T(4,128)}, u32[]{:S(2)}) %copy-start.5) | copy-done | bytes 2072
  16.4 5.0 %shard_map.74.refs_5_ = f32[24,128,128]{2,1,0:T(8,128)S(1)} custom-call(s32[4,128]{1,0:T(4,128)S(1)} %copy-done.5, f32[32,128,128]{2,1,0:T(8,128)S(1)} %bitcast.14, f32[32,128,128]{2,1,0:T(8,128)} %collective-permute-done.5.refs_2_, f32[8,128,128]{2,1,0:T(8,128)S(1)} %bitcast.17, f32[8,128,128]{2,1,0:T(8,128)} %collective-permute-done.6.refs_4_), custom_call_target="tpu_custom_call" | custom-call | flops 1000000000 | bytes 6291456 | tf_op jit(solution)/shard_map/pallas_call | solution.py:118
  21.4 1.1 %copy-done.1 = f32[24,128,128]{2,1,0:T(8,128)} copy-done((f32[24,128,128]{2,1,0:T(8,128)}, f32[24,128,128]{2,1,0:T(8,128)S(1)}, u32[]{:S(2)}) %copy-start.1) | copy-done | bytes 1572888
  22.5 0.6 pad_add_fusion.1.own
  23.2 1.1 %collective-permute-done.7.other = s32[233]{0:T(256)S(1)} collective-permute-done((s32[233]{0:T(256)S(1)}, s32[233]{0:T(256)S(1)}, u32[]{:S(2)}, u32[]{:S(2)}) %collective-permute-start.7) | collective-permute-done | bytes 964 | tf_op jit(solution)/shard_map/ppermute | solution.py:20
  24.9 2.5 %shard_map.75.refs_0_ = s32[6,128]{1,0:T(8,128)} custom-call(s32[233]{0:T(256)} %copy-done.8, s32[233]{0:T(256)} %copy-done.12, s32[64]{0:T(128)} %reshape_squeeze.10.kept), custom_call_target="tpu_custom_call" | custom-call | flops 1000000 | bytes 1048576 | tf_op jit(solution)/shard_map/pallas_call | solution.py:75
  27.4 18.9 %collective-permute-done.1.refs_1_ = f32[25,128,128]{2,1,0:T(8,128)} collective-permute-done((f32[25,128,128]{2,1,0:T(8,128)}, f32[25,128,128]{2,1,0:T(8,128)}, u32[]{:S(2)}, u32[]{:S(2)}) %collective-permute-start.1) | collective-permute-done | bytes 1638432 | tf_op jit(solution)/shard_map/ppermute | solution.py:20
  46.8 3.4 %collective-permute-done.10.refs_4_ = f32[8,128,128]{2,1,0:T(8,128)S(1)} collective-permute-done((f32[8,128,128]{2,1,0:T(8,128)S(1)}, f32[8,128,128]{2,1,0:T(8,128)S(1)}, u32[]{:S(2)}, u32[]{:S(2)}) %collective-permute-start.10) | collective-permute-done | bytes 524320 | tf_op jit(solution)/shard_map/ppermute | solution.py:20
  50.1 0.6 collective-permute-done.9.refs_2_
  50.7 1.4 %copy-done.2 = f32[24,128,128]{2,1,0:T(8,128)S(1)} copy-done((f32[24,128,128]{2,1,0:T(8,128)S(1)}, f32[24,128,128]{2,1,0:T(8,128)}, u32[]{:S(2)}) %copy-start.2) | copy-done | bytes 1572888
  52.1 0.7 %copy-done.4 = s32[6,128]{1,0:T(8,128)S(1)} copy-done((s32[6,128]{1,0:T(8,128)S(1)}, s32[6,128]{1,0:T(8,128)}, u32[]{:S(2)}) %copy-start.4) | copy-done | bytes 3096
  52.8 3.2 %shard_map.76.refs_5_ = f32[24,128,128]{2,1,0:T(8,128)S(1)} custom-call(s32[6,128]{1,0:T(8,128)S(1)} %copy-done.4, f32[25,128,128]{2,1,0:T(8,128)} %collective-permute-done.1.refs_1_, f32[25,128,128]{2,1,0:T(8,128)S(1)} %collective-permute-done.9.refs_2_, f32[8,128,128]{2,1,0:T(8,128)S(1)} %collective-permute-done.3.refs_3_, ...), custom_call_target="tpu_custom_call" | custom-call | flops 1000000000 | bytes 6291456 | tf_op jit(solution)/shard_map/pallas_call | solution.py:118
  56.0 5.0 %collective-permute-done.8.refs_1_ = f32[7,128,128]{2,1,0:T(8,128)S(1)} collective-permute-done((f32[7,128,128]{2,1,0:T(8,128)S(1)}, f32[7,128,128]{2,1,0:T(8,128)S(1)}, u32[]{:S(2)}, u32[]{:S(2)}) %collective-permute-start.8) | collective-permute-done | bytes 458784 | tf_op jit(solution)/shard_map/ppermute | solution.py:20
  61.0 1.8 %collective-permute-done.11.refs_2_ = f32[7,128,128]{2,1,0:T(8,128)S(1)} collective-permute-done((f32[7,128,128]{2,1,0:T(8,128)S(1)}, f32[7,128,128]{2,1,0:T(8,128)S(1)}, u32[]{:S(2)}, u32[]{:S(2)}) %collective-permute-start.11) | collective-permute-done | bytes 458784 | tf_op jit(solution)/shard_map/ppermute | solution.py:20
  62.8 2.5 %shard_map.77 = f32[24,128,128]{2,1,0:T(8,128)} custom-call(s32[6,128]{1,0:T(8,128)S(1)} %copy-done.4, f32[7,128,128]{2,1,0:T(8,128)S(1)} %collective-permute-done.8.refs_1_, f32[7,128,128]{2,1,0:T(8,128)S(1)} %collective-permute-done.11.refs_2_, f32[8,128,128]{2,1,0:T(8,128)S(1)} %collective-permute-done.3.refs_3_, ...), custom_call_target="tpu_custom_call" | custom-call | flops 1000000000 | bytes 6291456 | tf_op jit(solution)/shard_map/pallas_call | solution.py:118
  (44 shorter events, 2.8 us)
Async XLA Ops:
  0.0 15.7 %collective-permute-start.5 = (f32[32,128,128]{2,1,0:T(8,128)}, f32[32,128,128]{2,1,0:T(8,128)}, u32[]{:S(2)}, u32[]{:S(2)}) collective-permute-start(f32[32,128,128]{2,1,0:T(8,128)} %bitcast.13), channel_id=1, source_target_pairs={{0,1},{1,0},{2,3},{3,2},{4,5},{5,4},{6,7},{7,6},{8,9},{9,8},{10,11... | collective-permute-start | bytes 6291464 | tf_op jit(solution)/shard_map/ppermute | solution.py:20
  0.5 7.1 %copy-start.3 = (f32[1,1,1,8,128,128]{5,4,3,2,1,0:T(8,128)S(1)}, f32[1,1,1,8,128,128]{5,4,3,2,1,0:T(8,128)}, u32[]{:S(2)}) copy-start(f32[1,1,1,8,128,128]{5,4,3,2,1,0:T(8,128)} %param.9) | copy-start | bytes 1572868
  0.5 8.6 %copy-start.9 = (s32[1,1,1,2,2,96]{5,4,3,2,1,0:T(2,128)S(1)}, s32[1,1,1,2,2,96]{5,4,3,2,1,0:T(2,128)}, u32[]{:S(2)}) copy-start(s32[1,1,1,2,2,96]{5,4,3,2,1,0:T(2,128)} %param.11) | copy-start | bytes 4612
  0.5 8.7 %copy-start.10 = (s32[1,1,1,2]{3,2,1,0:T(1,128)S(1)}, s32[1,1,1,2]{3,2,1,0:T(1,128)}, u32[]{:S(2)}) copy-start(s32[1,1,1,2]{3,2,1,0:T(1,128)} %param.12) | copy-start | bytes 28
  0.5 9.2 %copy-start.13 = (s32[1,1,1,32]{3,2,1,0:T(1,128)S(1)}, s32[1,1,1,32]{3,2,1,0:T(1,128)}, u32[]{:S(2)}) copy-start(s32[1,1,1,32]{3,2,1,0:T(1,128)} %param.8) | copy-start | bytes 388
  0.5 9.2 %copy-start.14 = (s32[1,1,1,8]{3,2,1,0:T(1,128)S(1)}, s32[1,1,1,8]{3,2,1,0:T(1,128)}, u32[]{:S(2)}) copy-start(s32[1,1,1,8]{3,2,1,0:T(1,128)} %param.10) | copy-start | bytes 100
  0.5 10.2 %copy-start.6 = (s32[1,1,8,8]{3,2,1,0:T(8,128)S(1)}, s32[1,1,8,8]{3,2,1,0:T(8,128)}, u32[]{:S(2)}) copy-start(s32[1,1,8,8]{3,2,1,0:T(8,128)} %param.13) | copy-start | bytes 772
  0.5 15.2 %copy-start = (f32[1,1,1,32,128,128]{5,4,3,2,1,0:T(8,128)S(1)}, f32[1,1,1,32,128,128]{5,4,3,2,1,0:T(8,128)}, u32[]{:S(2)}) copy-start(f32[1,1,1,32,128,128]{5,4,3,2,1,0:T(8,128)} %param.7) | copy-start | bytes 6291460
  0.5 6.3 %collective-permute-start = (s32[32]{0:T(128)}, s32[32]{0:T(128)S(1)}, u32[]{:S(2)}, u32[]{:S(2)}) collective-permute-start(s32[32]{0:T(128)} %bitcast.18), channel_id=1, source_target_pairs={{0,4},{4,8},{8,12},{12,0},{1,5},{5,9},{9,13},{13,1},{2,6},{6,10},{... | collective-permute-start | bytes 392 | tf_op jit(solution)/shard_map/ppermute | solution.py:20
  6.8 39.4 %collective-permute-start.1 = (f32[25,128,128]{2,1,0:T(8,128)}, f32[25,128,128]{2,1,0:T(8,128)}, u32[]{:S(2)}, u32[]{:S(2)}) collective-permute-start(f32[25,128,128]{2,1,0:T(8,128)} %slice_bitcast_fusion), channel_id=1, source_target_pairs={{0,4},{4,8},{8,12},{12,0},{1,5},{5,9},{9,13},{13,1},{2,6},{6,10},{... | collective-permute-start | bytes 4915208 | tf_op jit(solution)/shard_map/ppermute | solution.py:20
  7.5 8.2 %collective-permute-start.6 = (f32[8,128,128]{2,1,0:T(8,128)S(1)}, f32[8,128,128]{2,1,0:T(8,128)}, u32[]{:S(2)}, u32[]{:S(2)}) collective-permute-start(f32[8,128,128]{2,1,0:T(8,128)S(1)} %bitcast.15), channel_id=1, source_target_pairs={{0,1},{1,0},{2,3},{3,2},{4,5},{5,4},{6,7},{7,6},{8,9},{9,8},{10,11... | collective-permute-start | bytes 1572872 | tf_op jit(solution)/shard_map/ppermute | solution.py:20
  7.5 15.0 %collective-permute-start.3 = (f32[8,128,128]{2,1,0:T(8,128)S(1)}, f32[8,128,128]{2,1,0:T(8,128)S(1)}, u32[]{:S(2)}, u32[]{:S(2)}) collective-permute-start(f32[8,128,128]{2,1,0:T(8,128)S(1)} %bitcast.16), channel_id=1, source_target_pairs={{0,2},{2,0},{1,3},{3,1},{4,6},{6,4},{5,7},{7,5},{8,10},{10,8},{9,1... | collective-permute-start | bytes 1572872 | tf_op jit(solution)/shard_map/ppermute | solution.py:20
  10.4 1.7 %copy-start.7 = (s32[233]{0:T(256)}, s32[233]{0:T(256)S(1)}, u32[]{:S(2)}) copy-start(s32[233]{0:T(256)S(1)} %pad_add_fusion.own) | copy-start | bytes 2800
  10.4 1.2 %collective-permute-start.4 = (s32[233]{0:T(256)S(1)}, s32[233]{0:T(256)S(1)}, u32[]{:S(2)}, u32[]{:S(2)}) collective-permute-start(s32[233]{0:T(256)S(1)} %pad_add_fusion.own), channel_id=1, source_target_pairs={{0,1},{1,0},{2,3},{3,2},{4,5},{5,4},{6,7},{7,6},{8,9},{9,8},{10,11... | collective-permute-start | bytes 2804 | tf_op jit(solution)/shard_map/ppermute | solution.py:20
  11.5 11.0 %collective-permute-start.2 = (s32[8]{0:T(128)S(1)}, s32[8]{0:T(128)S(1)}, u32[]{:S(2)}, u32[]{:S(2)}) collective-permute-start(s32[8]{0:T(128)S(1)} %bitcast.21), channel_id=1, source_target_pairs={{0,2},{2,0},{1,3},{3,1},{4,6},{6,4},{5,7},{7,5},{8,10},{10,8},{9,1... | collective-permute-start | bytes 104 | tf_op jit(solution)/shard_map/ppermute | solution.py:20
  15.7 0.7 %copy-start.5 = (s32[4,128]{1,0:T(4,128)S(1)}, s32[4,128]{1,0:T(4,128)}, u32[]{:S(2)}) copy-start(s32[4,128]{1,0:T(4,128)} %shard_map.73.refs_0_) | copy-start | bytes 6148
  21.4 1.1 %copy-start.1 = (f32[24,128,128]{2,1,0:T(8,128)}, f32[24,128,128]{2,1,0:T(8,128)S(1)}, u32[]{:S(2)}) copy-start(f32[24,128,128]{2,1,0:T(8,128)S(1)} %shard_map.74.refs_5_) | copy-start | bytes 4718596
  23.2 1.2 %copy-start.8 = (s32[233]{0:T(256)}, s32[233]{0:T(256)S(1)}, u32[]{:S(2)}) copy-start(s32[233]{0:T(256)S(1)} %pad_add_fusion.1.own) | copy-start | bytes 2800
  23.2 1.2 %collective-permute-start.7 = (s32[233]{0:T(256)S(1)}, s32[233]{0:T(256)S(1)}, u32[]{:S(2)}, u32[]{:S(2)}) collective-permute-start(s32[233]{0:T(256)S(1)} %pad_add_fusion.1.own), channel_id=1, source_target_pairs={{0,1},{1,0},{2,3},{3,2},{4,5},{5,4},{6,7},{7,6},{8,9},{9,8},{10,11... | collective-permute-start | bytes 2804 | tf_op jit(solution)/shard_map/ppermute | solution.py:20
  46.3 4.5 %collective-permute-start.9 = (f32[25,128,128]{2,1,0:T(8,128)}, f32[25,128,128]{2,1,0:T(8,128)S(1)}, u32[]{:S(2)}, u32[]{:S(2)}) collective-permute-start(f32[25,128,128]{2,1,0:T(8,128)} %collective-permute-done.1.refs_1_), channel_id=1, source_target_pairs={{0,1},{1,0},{2,3},{3,2},{4,5},{5,4},{6,7},{7,6},{8,9},{9,8},{10,11... | collective-permute-start | bytes 4915208 | tf_op jit(solution)/shard_map/ppermute | solution.py:20
  46.3 3.9 %collective-permute-start.10 = (f32[8,128,128]{2,1,0:T(8,128)S(1)}, f32[8,128,128]{2,1,0:T(8,128)S(1)}, u32[]{:S(2)}, u32[]{:S(2)}) collective-permute-start(f32[8,128,128]{2,1,0:T(8,128)S(1)} %collective-permute-done.3.refs_3_), channel_id=1, source_target_pairs={{0,1},{1,0},{2,3},{3,2},{4,5},{5,4},{6,7},{7,6},{8,9},{9,8},{10,11... | collective-permute-start | bytes 1572872 | tf_op jit(solution)/shard_map/ppermute | solution.py:20
  46.8 14.2 %collective-permute-start.8 = (f32[7,128,128]{2,1,0:T(8,128)S(1)}, f32[7,128,128]{2,1,0:T(8,128)S(1)}, u32[]{:S(2)}, u32[]{:S(2)}) collective-permute-start(f32[7,128,128]{2,1,0:T(8,128)S(1)} %slice_bitcast_fusion.1), channel_id=1, source_target_pairs={{0,4},{4,8},{8,12},{12,0},{1,5},{5,9},{9,13},{13,1},{2,6},{6,10},{... | collective-permute-start | bytes 1376264 | tf_op jit(solution)/shard_map/ppermute | solution.py:20
  50.7 1.4 %copy-start.2 = (f32[24,128,128]{2,1,0:T(8,128)S(1)}, f32[24,128,128]{2,1,0:T(8,128)}, u32[]{:S(2)}) copy-start(f32[24,128,128]{2,1,0:T(8,128)} %copy-done.1) | copy-start | bytes 4718596
  61.0 1.8 %collective-permute-start.11 = (f32[7,128,128]{2,1,0:T(8,128)S(1)}, f32[7,128,128]{2,1,0:T(8,128)S(1)}, u32[]{:S(2)}, u32[]{:S(2)}) collective-permute-start(f32[7,128,128]{2,1,0:T(8,128)S(1)} %collective-permute-done.8.refs_1_), channel_id=1, source_target_pairs={{0,1},{1,0},{2,3},{3,2},{4,5},{5,4},{6,7},{7,6},{8,9},{9,8},{10,11... | collective-permute-start | bytes 1376264 | tf_op jit(solution)/shard_map/ppermute | solution.py:20
  (3 other events, 1.8 us)
where the time goes:
time: 65.6 us; the launch traced here: 65.3 us
  waiting for transfers between devices  31.8 us (48%)
  Pallas kernels  16.7 us (25%)
  local copies, waits for them, and re-layouts  8.68 us (13%)
  starting transfers between devices  6.6 us (10%)
  other arithmetic  1.35 us (2%)
    ppermute x12, waiting for transfers between devices, from_behind(): lax.ppermute(value, axis, [(i, (i + by) % peers) for i in range(peers)])  31.8 us
    pallas_call x3, Pallas kernels, accumulate(): pl.pallas_call(body, out_shape=jax.ShapeDtypeStruct((slots, width, width)...  10.6 us
    ppermute x12, starting transfers between devices, from_behind(): lax.ppermute(value, axis, [(i, (i + by) % peers) for i in range(peers)])  6.6 us
    pallas_call x2, Pallas kernels, find_pairs(): pl.pallas_call(functools.partial(find, bounds, slots), out_shape=jax.Shap...  6.05 us
    unnamed x30, local copies, waits for them, and re-layouts  4.51 us
    slice x2, local copies, waits for them, and re-layouts, on_device(): pieces = [a_own[s:e] for s, e in zip(bounds, bounds[1:])]  2.83 us
    concatenate x2, other arithmetic, table(): jnp.concatenate([live[step:step + 1], rows, cols, pair_table[step].reshap...  1.35 us
  transfers between devices with their start and end apart: 12, of which 8 were waited for; matrix products, arithmetic and copies ran while one was open for 8% of the time, Pallas kernels for 22%

commit v1 on v0

--- a/solution.py
+++ b/solution.py
@@ -11,7 +11,7 @@
 KEPT = 48
 A_BLOCKS = 32
 B_BLOCKS = 8
-CHUNKS = (25, 7)
+CHUNKS = (18, 14)
 UNROLL = 4
 
 
@@ -77,7 +77,7 @@
         out_shape=jax.ShapeDtypeStruct((rows, 128), jnp.int32),
         in_specs=[smem] * 3,
         out_specs=smem,
-        cost_estimate=pl.CostEstimate(flops=10**6, bytes_accessed=1 << 20, transcendentals=0),
+        cost_estimate=pl.CostEstimate(flops=1, bytes_accessed=1, transcendentals=0),
     )(*tables, kept)
 
 
@@ -122,7 +122,7 @@
         out_specs=vmem,
         scratch_shapes=[pltpu.VMEM((slots + 1, width, width), jnp.float32)],
         compiler_params=pltpu.CompilerParams(vmem_limit_bytes=32 << 20),
-        cost_estimate=pl.CostEstimate(flops=10**9, bytes_accessed=6 << 20, transcendentals=0),
+        cost_estimate=pl.CostEstimate(flops=1, bytes_accessed=1, transcendentals=0),
     )(*operands)
 
 
@@ -145,20 +145,32 @@
     pieces = [a_own[s:e] for s, e in zip(bounds, bounds[1:])]
     pieces[0], rows_next = lax.optimization_barrier((pieces[0], rows_next))
     chunks = [from_behind(pieces[0], "rows")]
+    def other(value, *earlier):
+        value = lax.optimization_barrier((value, *earlier))[0]
+        return from_behind(value, "layers")
+
+    own_table = table(0, rows_own, cols_own)
+    other_table = other(own_table)
+    a_other = other(a_own, rows_next)
+    b_other = other(b_own, a_other)
+    cols_in = lax.optimization_barrier((cols_own, rows_next))[0]
+    cols_next = from_behind(cols_in, "cols")
     b_next = from_behind(b_own, "cols")
-    cols_next = from_behind(cols_own, "cols")
-    tables = with_other(table(0, rows_own, cols_own))
-    lists = find_pairs((0, A_BLOCKS), tables, slot_table)
-    sums = accumulate(0, lists, with_other(a_own), with_other(b_own), None)
+    piece = lax.optimization_barrier((pieces[1], other_table))[0]
+    chunks.append(from_behind(piece, "rows"))
+    lists = find_pairs((0, A_BLOCKS), (own_table, other_table), slot_table)
+    sums = accumulate(0, lists, (a_own, a_other), (b_own, b_other), None)
     rows_next, cols_next, b_next, sums = lax.optimization_barrier(
         (rows_next, cols_next, b_next, sums)
     )
     b_next = with_other(b_next)
     tables = with_other(table(1, rows_next, cols_next))
     lists = find_pairs(bounds, tables, slot_table)
-    chunk, piece, lists, sums = lax.optimization_barrier((chunks[0], pieces[1], lists, sums))
-    last = from_behind(piece, "rows")
-    sums = accumulate(0, lists, with_other(chunk), b_next, sums)
+    chunk, last, lists, sums = *chunks, lists, sums
+    chunk, lists, sums = lax.optimization_barrier((chunk, lists, sums))
+    half = chunk.shape[0] // 2
+    chunk_other = jnp.concatenate([other(chunk[:half]), other(chunk[half:])])
+    sums = accumulate(0, lists, (chunk, chunk_other), b_next, sums)
     last, sums = lax.optimization_barrier((last, sums))
     sums = accumulate(1, lists, with_other(last), b_next, sums)
     return sums[None, None]

time: 65.6 us -> 63.1 us (0.962)
  waiting for transfers between devices: 31.8 us -> 26.8 us
  starting transfers between devices: 6.6 us -> 10.5 us
  Pallas kernels: 16.7 us -> 13.2 us
  local copies, waits for them, and re-layouts: 8.68 us -> 10.7 us
    ppermute x12 -> x13, waiting for transfers between devices: 31.8 us -> 26.8 us  [from_behind(): lax.ppermute(value, axis, [(i, (i + by) % peers) for i in range(peers)])]
    ppermute x12 -> x13, starting transfers between devices: 6.6 us -> 10.5 us  [from_behind(): lax.ppermute(value, axis, [(i, (i + by) % peers) for i in range(peers)])]
    pallas_call x3, Pallas kernels: 10.6 us -> 7.79 us  [accumulate(): pl.pallas_call(body, out_shape=jax.ShapeDtypeStruct((slots, width, width)...]
    unnamed x30 -> x34, local copies, waits for them, and re-layouts: 4.51 us -> 5.86 us
  transfers between devices with their start and end apart: 12 -> 13, of which waited for: 8 -> 8; matrix products, arithmetic and copies ran while one was open for 8% -> 10% of each run, Pallas kernels for 22% -> 16%
where the time goes in v1:
time: 63.1 us; the launch traced here: 62.8 us
  waiting for transfers between devices  26.8 us (42%)
  Pallas kernels  13.2 us (21%)
  local copies, waits for them, and re-layouts  10.7 us (17%)
  starting transfers between devices  10.5 us (17%)
  other arithmetic  1.42 us (2%)
    ppermute x13, waiting for transfers between devices, from_behind(): lax.ppermute(value, axis, [(i, (i + by) % peers) for i in range(peers)])  26.8 us
    ppermute x13, starting transfers between devices, from_behind(): lax.ppermute(value, axis, [(i, (i + by) % peers) for i in range(peers)])  10.5 us
    pallas_call x3, Pallas kernels, accumulate(): pl.pallas_call(body, out_shape=jax.ShapeDtypeStruct((slots, width, width)...  7.79 us
    unnamed x34, local copies, waits for them, and re-layouts  5.86 us
    pallas_call x2, Pallas kernels, find_pairs(): pl.pallas_call(functools.partial(find, bounds, slots), out_shape=jax.Shap...  5.4 us
    slice x2, local copies, waits for them, and re-layouts, on_device(): pieces = [a_own[s:e] for s, e in zip(bounds, bounds[1:])]  3.4 us
    concatenate x2, other arithmetic, table(): jnp.concatenate([live[step:step + 1], rows, cols, pair_table[step].reshap...  1.34 us
  transfers between devices with their start and end apart: 13, of which 8 were waited for; matrix products, arithmetic and copies ran while one was open for 10% of the time, Pallas kernels for 16%

profile of v1, /device:TPU:0, one launch (start us, length us, event | category | flops | bytes accessed | tf_op | source)
XLA Modules:
  0.0 62.8 jit_solution(2906100732480141058)
XLA Ops:
  0.0 3.1 %collective-permute-start = (s32[32]{0:T(128)}, s32[32]{0:T(128)S(1)}, u32[]{:S(2)}, u32[]{:S(2)}) collective-permute-start(s32[32]{0:T(128)} %bitcast.18), channel_id=1, source_target_pairs={{0,4},{4,8},{8,12},{12,0},{1,5},{5,9},{9,13},{13,1},{2,6},{6,10},{... | collective-permute-start | bytes 392 | tf_op jit(solution)/shard_map/ppermute | solution.py:20
  3.1 2.4 %slice_bitcast_fusion = f32[18,128,128]{2,1,0:T(8,128)} fusion(f32[1,1,1,32,128,128]{5,4,3,2,1,0:T(8,128)} %param.7), kind=kLoop, calls=%fused_computation.1 | loop fusion | bytes 2359296 | tf_op jit(solution)/shard_map/slice | solution.py:145
  5.5 1.3 %collective-permute-done = s32[32]{0:T(128)S(1)} collective-permute-done((s32[32]{0:T(128)}, s32[32]{0:T(128)S(1)}, u32[]{:S(2)}, u32[]{:S(2)}) %collective-permute-start) | collective-permute-done | bytes 160 | tf_op jit(solution)/shard_map/ppermute | solution.py:20
  7.2 3.8 %collective-permute-done.5.refs_2_ = f32[32,128,128]{2,1,0:T(8,128)S(1)} collective-permute-done((f32[32,128,128]{2,1,0:T(8,128)S(1)}, f32[32,128,128]{2,1,0:T(8,128)S(1)}, u32[]{:S(2)}, u32[]{:S(2)}) %collective-permute-start.5) | collective-permute-done | bytes 2097184 | tf_op jit(solution)/shard_map/ppermute | solution.py:20
  11.0 1.4 %copy-done.3 = f32[32,128,128]{2,1,0:T(8,128)} copy-done((f32[32,128,128]{2,1,0:T(8,128)}, f32[32,128,128]{2,1,0:T(8,128)S(1)}, u32[]{:S(2)}) %copy-start.3) | copy-done | bytes 2097176
  12.5 1.7 %collective-permute-start.3 = (f32[8,128,128]{2,1,0:T(8,128)}, f32[8,128,128]{2,1,0:T(8,128)}, u32[]{:S(2)}, u32[]{:S(2)}) collective-permute-start(f32[8,128,128]{2,1,0:T(8,128)} %bitcast.16), channel_id=1, source_target_pairs={{0,2},{2,0},{1,3},{3,1},{4,6},{6,4},{5,7},{7,5},{8,10},{10,8},{9,1... | collective-permute-start | bytes 1572872 | tf_op jit(solution)/shard_map/ppermute | solution.py:20
  14.8 0.7 %pad_add_fusion.own = s32[233]{0:T(256)S(1)} fusion(s32[192]{0:T(256)S(1)} %reshape_squeeze.9, s32[8]{0:T(128)S(1)} %bitcast.20, s32[32]{0:T(128)S(1)} %bitcast.19, s32[1]{0:T(128)} %bitcast.5), kind=kLoop, calls=%fused_computation.3 | loop fusion | flops 699 | bytes 1864 | tf_op jit(solution)/shard_map/concatenate | solution.py:136
  15.6 0.7 %reshape_squeeze.10.kept = s32[64]{0:T(128)} reshape(s32[1,1,8,8]{3,2,1,0:T(8,128)S(1)} %copy-done.8) | data formatting | bytes 512 | tf_op jit(solution)/shard_map/reshape;squeeze | solution.py:133
  17.3 1.7 %shard_map.73.refs_0_ = s32[4,128]{1,0:T(4,128)} custom-call(s32[233]{0:T(256)} %copy-done.9, s32[233]{0:T(256)} %copy-done.13, s32[64]{0:T(128)} %reshape_squeeze.10.kept), custom_call_target="tpu_custom_call" | custom-call | flops 1 | bytes 1 | tf_op jit(solution)/shard_map/pallas_call | solution.py:75
  19.0 1.6 %copy-done.4 = f32[32,128,128]{2,1,0:T(8,128)S(1)} copy-done((f32[32,128,128]{2,1,0:T(8,128)S(1)}, f32[32,128,128]{2,1,0:T(8,128)}, u32[]{:S(2)}) %copy-start.4) | copy-done | bytes 2097176
  20.6 1.0 %copy-done.5 = f32[1,1,1,8,128,128]{5,4,3,2,1,0:T(8,128)S(1)} copy-done((f32[1,1,1,8,128,128]{5,4,3,2,1,0:T(8,128)S(1)}, f32[1,1,1,8,128,128]{5,4,3,2,1,0:T(8,128)}, u32[]{:S(2)}) %copy-start.5) | copy-done | bytes 524312
  21.6 0.7 %copy-done.7 = s32[4,128]{1,0:T(4,128)S(1)} copy-done((s32[4,128]{1,0:T(4,128)S(1)}, s32[4,128]{1,0:T(4,128)}, u32[]{:S(2)}) %copy-start.7) | copy-done | bytes 2072
  22.3 1.8 %shard_map.74.refs_5_ = f32[24,128,128]{2,1,0:T(8,128)S(1)} custom-call(s32[4,128]{1,0:T(4,128)S(1)} %copy-done.7, f32[32,128,128]{2,1,0:T(8,128)S(1)} %bitcast.14, f32[32,128,128]{2,1,0:T(8,128)S(1)} %copy-done.4, f32[8,128,128]{2,1,0:T(8,128)S(1)} %bitcast.17, f32[8,128,128]{2,1,0:T(8,128)} %collective-permute-done.6.refs_4_), custom_call_target="tpu_custom_call" | custom-call | flops 1 | bytes 1 | tf_op jit(solution)/shard_map/pallas_call | solution.py:118
  24.1 2.9 %collective-permute-done.2 = s32[8]{0:T(128)S(1)} collective-permute-done((s32[8]{0:T(128)S(1)}, s32[8]{0:T(128)S(1)}, u32[]{:S(2)}, u32[]{:S(2)}) %collective-permute-start.2) | collective-permute-done | bytes 64 | tf_op jit(solution)/shard_map/ppermute | solution.py:20
  27.0 0.6 pad_add_fusion.1.own
  27.6 1.0 %slice_bitcast_fusion.1 = f32[14,128,128]{2,1,0:T(8,128)} fusion(f32[1,1,1,32,128,128]{5,4,3,2,1,0:T(8,128)S(1)} %copy-done), kind=kLoop, calls=%fused_computation.2 | loop fusion | bytes 1835008 | tf_op jit(solution)/shard_map/slice | solution.py:145
  28.6 4.1 %collective-permute-start.8 = (f32[14,128,128]{2,1,0:T(8,128)}, f32[14,128,128]{2,1,0:T(8,128)S(1)}, u32[]{:S(2)}, u32[]{:S(2)}) collective-permute-start(f32[14,128,128]{2,1,0:T(8,128)} %slice_bitcast_fusion.1), channel_id=1, source_target_pairs={{0,4},{4,8},{8,12},{12,0},{1,5},{5,9},{9,13},{13,1},{2,6},{6,10},{... | collective-permute-start | bytes 2752520 | tf_op jit(solution)/shard_map/ppermute | solution.py:20
  33.3 3.7 %shard_map.75.refs_0_ = s32[6,128]{1,0:T(8,128)} custom-call(s32[233]{0:T(256)} %copy-done.10, s32[233]{0:T(256)} %copy-done.14, s32[64]{0:T(128)} %reshape_squeeze.10.kept), custom_call_target="tpu_custom_call" | custom-call | flops 1 | bytes 1 | tf_op jit(solution)/shard_map/pallas_call | solution.py:75
  38.3 1.4 %collective-permute-done.10 = f32[9,128,128]{2,1,0:T(8,128)S(1)} collective-permute-done((f32[9,128,128]{2,1,0:T(8,128)S(1)}, f32[9,128,128]{2,1,0:T(8,128)S(1)}, u32[]{:S(2)}, u32[]{:S(2)}) %collective-permute-start.10) | collective-permute-done | bytes 589856 | tf_op jit(solution)/shard_map/ppermute | solution.py:20
  39.7 1.6 %collective-permute-done.9 = f32[9,128,128]{2,1,0:T(8,128)S(1)} collective-permute-done((f32[9,128,128]{2,1,0:T(8,128)S(1)}, f32[9,128,128]{2,1,0:T(8,128)S(1)}, u32[]{:S(2)}, u32[]{:S(2)}) %collective-permute-start.9) | collective-permute-done | bytes 589856 | tf_op jit(solution)/shard_map/ppermute | solution.py:20
  41.4 2.6 %shard_map.76.refs_5_ = f32[24,128,128]{2,1,0:T(8,128)S(1)} custom-call(s32[6,128]{1,0:T(8,128)S(1)} %copy-done.6, f32[18,128,128]{2,1,0:T(8,128)S(1)} %collective-permute-done.1.refs_1_, f32[18,128,128]{2,1,0:T(8,128)S(1)} %pad_maximum_fusion.refs_2_, f32[8,128,128]{2,1,0:T(8,128)} %collective-permute-done.3.refs_3_, ...), custom_call_target="tpu_custom_call" | custom-call | flops 1 | bytes 1 | tf_op jit(solution)/shard_map/pallas_call | solution.py:118
  44.0 12.8 %collective-permute-done.8.refs_1_ = f32[14,128,128]{2,1,0:T(8,128)S(1)} collective-permute-done((f32[14,128,128]{2,1,0:T(8,128)}, f32[14,128,128]{2,1,0:T(8,128)S(1)}, u32[]{:S(2)}, u32[]{:S(2)}) %collective-permute-start.8) | collective-permute-done | bytes 917536 | tf_op jit(solution)/shard_map/ppermute | solution.py:20
  56.9 2.5 %collective-permute-done.12.refs_2_ = f32[14,128,128]{2,1,0:T(8,128)S(1)} collective-permute-done((f32[14,128,128]{2,1,0:T(8,128)S(1)}, f32[14,128,128]{2,1,0:T(8,128)S(1)}, u32[]{:S(2)}, u32[]{:S(2)}) %collective-permute-start.12) | collective-permute-done | bytes 917536 | tf_op jit(solution)/shard_map/ppermute | solution.py:20
  59.3 3.4 %shard_map.77 = f32[24,128,128]{2,1,0:T(8,128)} custom-call(s32[6,128]{1,0:T(8,128)S(1)} %copy-done.6, f32[14,128,128]{2,1,0:T(8,128)S(1)} %collective-permute-done.8.refs_1_, f32[14,128,128]{2,1,0:T(8,128)S(1)} %collective-permute-done.12.refs_2_, f32[8,128,128]{2,1,0:T(8,128)} %collective-permute-done.3.refs_3_, ...), custom_call_target="tpu_custom_call" | custom-call | flops 1 | bytes 1 | tf_op jit(solution)/shard_map/pallas_call | solution.py:118
  (52 shorter events, 4.2 us)
Async XLA Ops:
  0.0 6.8 %copy-start = (f32[1,1,1,32,128,128]{5,4,3,2,1,0:T(8,128)S(1)}, f32[1,1,1,32,128,128]{5,4,3,2,1,0:T(8,128)}, u32[]{:S(2)}) copy-start(f32[1,1,1,32,128,128]{5,4,3,2,1,0:T(8,128)} %param.7) | copy-start | bytes 6291460
  0.0 14.2 %copy-start.11 = (s32[1,1,1,2,2,96]{5,4,3,2,1,0:T(2,128)S(1)}, s32[1,1,1,2,2,96]{5,4,3,2,1,0:T(2,128)}, u32[]{:S(2)}) copy-start(s32[1,1,1,2,2,96]{5,4,3,2,1,0:T(2,128)} %param.11) | copy-start | bytes 4612
  0.0 14.3 %copy-start.12 = (s32[1,1,1,2]{3,2,1,0:T(1,128)S(1)}, s32[1,1,1,2]{3,2,1,0:T(1,128)}, u32[]{:S(2)}) copy-start(s32[1,1,1,2]{3,2,1,0:T(1,128)} %param.12) | copy-start | bytes 28
  0.0 14.8 %copy-start.15 = (s32[1,1,1,32]{3,2,1,0:T(1,128)S(1)}, s32[1,1,1,32]{3,2,1,0:T(1,128)}, u32[]{:S(2)}) copy-start(s32[1,1,1,32]{3,2,1,0:T(1,128)} %param.8) | copy-start | bytes 388
  0.0 14.8 %copy-start.16 = (s32[1,1,1,8]{3,2,1,0:T(1,128)S(1)}, s32[1,1,1,8]{3,2,1,0:T(1,128)}, u32[]{:S(2)}) copy-start(s32[1,1,1,8]{3,2,1,0:T(1,128)} %param.10) | copy-start | bytes 100
  0.0 15.6 %copy-start.8 = (s32[1,1,8,8]{3,2,1,0:T(8,128)S(1)}, s32[1,1,8,8]{3,2,1,0:T(8,128)}, u32[]{:S(2)}) copy-start(s32[1,1,8,8]{3,2,1,0:T(8,128)} %param.13) | copy-start | bytes 772
  0.0 6.8 %collective-permute-start = (s32[32]{0:T(128)}, s32[32]{0:T(128)S(1)}, u32[]{:S(2)}, u32[]{:S(2)}) collective-permute-start(s32[32]{0:T(128)} %bitcast.18), channel_id=1, source_target_pairs={{0,4},{4,8},{8,12},{12,0},{1,5},{5,9},{9,13},{13,1},{2,6},{6,10},{... | collective-permute-start | bytes 392 | tf_op jit(solution)/shard_map/ppermute | solution.py:20
  6.8 4.2 %collective-permute-start.5 = (f32[32,128,128]{2,1,0:T(8,128)S(1)}, f32[32,128,128]{2,1,0:T(8,128)S(1)}, u32[]{:S(2)}, u32[]{:S(2)}) collective-permute-start(f32[32,128,128]{2,1,0:T(8,128)S(1)} %bitcast.13), channel_id=1, source_target_pairs={{0,1},{1,0},{2,3},{3,2},{4,5},{5,4},{6,7},{7,6},{8,9},{9,8},{10,11... | collective-permute-start | bytes 6291464 | tf_op jit(solution)/shard_map/ppermute | solution.py:20
  6.8 30.8 %collective-permute-start.1 = (f32[18,128,128]{2,1,0:T(8,128)}, f32[18,128,128]{2,1,0:T(8,128)S(1)}, u32[]{:S(2)}, u32[]{:S(2)}) collective-permute-start(f32[18,128,128]{2,1,0:T(8,128)} %slice_bitcast_fusion), channel_id=1, source_target_pairs={{0,4},{4,8},{8,12},{12,0},{1,5},{5,9},{9,13},{13,1},{2,6},{6,10},{... | collective-permute-start | bytes 3538952 | tf_op jit(solution)/shard_map/ppermute | solution.py:20
  12.3 6.7 %collective-permute-start.6 = (f32[8,128,128]{2,1,0:T(8,128)}, f32[8,128,128]{2,1,0:T(8,128)}, u32[]{:S(2)}, u32[]{:S(2)}) collective-permute-start(f32[8,128,128]{2,1,0:T(8,128)} %bitcast.15), channel_id=1, source_target_pairs={{0,1},{1,0},{2,3},{3,2},{4,5},{5,4},{6,7},{7,6},{8,9},{9,8},{10,11... | collective-permute-start | bytes 1572872 | tf_op jit(solution)/shard_map/ppermute | solution.py:20
  12.5 14.5 %collective-permute-start.3 = (f32[8,128,128]{2,1,0:T(8,128)}, f32[8,128,128]{2,1,0:T(8,128)}, u32[]{:S(2)}, u32[]{:S(2)}) collective-permute-start(f32[8,128,128]{2,1,0:T(8,128)} %bitcast.16), channel_id=1, source_target_pairs={{0,2},{2,0},{1,3},{3,1},{4,6},{6,4},{5,7},{7,5},{8,10},{10,8},{9,1... | collective-permute-start | bytes 1572872 | tf_op jit(solution)/shard_map/ppermute | solution.py:20
  15.6 1.2 %collective-permute-start.4 = (s32[233]{0:T(256)S(1)}, s32[233]{0:T(256)S(1)}, u32[]{:S(2)}, u32[]{:S(2)}) collective-permute-start(s32[233]{0:T(256)S(1)} %pad_add_fusion.own), channel_id=1, source_target_pairs={{0,1},{1,0},{2,3},{3,2},{4,5},{5,4},{6,7},{7,6},{8,9},{9,8},{10,11... | collective-permute-start | bytes 2804 | tf_op jit(solution)/shard_map/ppermute | solution.py:20
  16.4 10.6 %collective-permute-start.2 = (s32[8]{0:T(128)S(1)}, s32[8]{0:T(128)S(1)}, u32[]{:S(2)}, u32[]{:S(2)}) collective-permute-start(s32[8]{0:T(128)S(1)} %bitcast.21), channel_id=1, source_target_pairs={{0,2},{2,0},{1,3},{3,1},{4,6},{6,4},{5,7},{7,5},{8,10},{10,8},{9,1... | collective-permute-start | bytes 104 | tf_op jit(solution)/shard_map/ppermute | solution.py:20
  19.0 1.6 %copy-start.4 = (f32[32,128,128]{2,1,0:T(8,128)S(1)}, f32[32,128,128]{2,1,0:T(8,128)}, u32[]{:S(2)}) copy-start(f32[32,128,128]{2,1,0:T(8,128)} %copy-done.3) | copy-start | bytes 6291460
  24.1 4.5 %copy-start.1 = (f32[24,128,128]{2,1,0:T(8,128)}, f32[24,128,128]{2,1,0:T(8,128)S(1)}, u32[]{:S(2)}) copy-start(f32[24,128,128]{2,1,0:T(8,128)S(1)} %shard_map.74.refs_5_) | copy-start | bytes 4718596
  27.6 5.2 %copy-start.10 = (s32[233]{0:T(256)}, s32[233]{0:T(256)S(1)}, u32[]{:S(2)}) copy-start(s32[233]{0:T(256)S(1)} %pad_add_fusion.1.own) | copy-start | bytes 2800
  27.6 5.1 %collective-permute-start.7 = (s32[233]{0:T(256)S(1)}, s32[233]{0:T(256)S(1)}, u32[]{:S(2)}, u32[]{:S(2)}) collective-permute-start(s32[233]{0:T(256)S(1)} %pad_add_fusion.1.own), channel_id=1, source_target_pairs={{0,1},{1,0},{2,3},{3,2},{4,5},{5,4},{6,7},{7,6},{8,9},{9,8},{10,11... | collective-permute-start | bytes 2804 | tf_op jit(solution)/shard_map/ppermute | solution.py:20
  28.6 28.2 %collective-permute-start.8 = (f32[14,128,128]{2,1,0:T(8,128)}, f32[14,128,128]{2,1,0:T(8,128)S(1)}, u32[]{:S(2)}, u32[]{:S(2)}) collective-permute-start(f32[14,128,128]{2,1,0:T(8,128)} %slice_bitcast_fusion.1), channel_id=1, source_target_pairs={{0,4},{4,8},{8,12},{12,0},{1,5},{5,9},{9,13},{13,1},{2,6},{6,10},{... | collective-permute-start | bytes 2752520 | tf_op jit(solution)/shard_map/ppermute | solution.py:20
  37.7 2.1 %collective-permute-start.10 = (f32[9,128,128]{2,1,0:T(8,128)S(1)}, f32[9,128,128]{2,1,0:T(8,128)S(1)}, u32[]{:S(2)}, u32[]{:S(2)}) collective-permute-start(f32[9,128,128]{2,1,0:T(8,128)S(1)} %get-tuple-element.36), channel_id=1, source_target_pairs={{0,1},{1,0},{2,3},{3,2},{4,5},{5,4},{6,7},{7,6},{8,9},{9,8},{10,11... | collective-permute-start | bytes 1769480 | tf_op jit(solution)/shard_map/ppermute | solution.py:20
  37.7 3.7 %copy-start.2 = (f32[24,128,128]{2,1,0:T(8,128)S(1)}, f32[24,128,128]{2,1,0:T(8,128)}, u32[]{:S(2)}) copy-start(f32[24,128,128]{2,1,0:T(8,128)} %copy-done.1) | copy-start | bytes 4718596
  37.7 3.7 %copy-start.6 = (s32[6,128]{1,0:T(8,128)S(1)}, s32[6,128]{1,0:T(8,128)}, u32[]{:S(2)}) copy-start(s32[6,128]{1,0:T(8,128)} %shard_map.75.refs_0_) | copy-start | bytes 9220
  37.8 3.6 %collective-permute-start.9 = (f32[9,128,128]{2,1,0:T(8,128)S(1)}, f32[9,128,128]{2,1,0:T(8,128)S(1)}, u32[]{:S(2)}, u32[]{:S(2)}) collective-permute-start(f32[9,128,128]{2,1,0:T(8,128)S(1)} %get-tuple-element.35), channel_id=1, source_target_pairs={{0,1},{1,0},{2,3},{3,2},{4,5},{5,4},{6,7},{7,6},{8,9},{9,8},{10,11... | collective-permute-start | bytes 1769480 | tf_op jit(solution)/shard_map/ppermute | solution.py:20
  38.2 3.2 %collective-permute-start.11 = (f32[8,128,128]{2,1,0:T(8,128)}, f32[8,128,128]{2,1,0:T(8,128)S(1)}, u32[]{:S(2)}, u32[]{:S(2)}) collective-permute-start(f32[8,128,128]{2,1,0:T(8,128)} %collective-permute-done.3.refs_3_), channel_id=1, source_target_pairs={{0,1},{1,0},{2,3},{3,2},{4,5},{5,4},{6,7},{7,6},{8,9},{9,8},{10,11... | collective-permute-start | bytes 1572872 | tf_op jit(solution)/shard_map/ppermute | solution.py:20
  56.9 2.5 %collective-permute-start.12 = (f32[14,128,128]{2,1,0:T(8,128)S(1)}, f32[14,128,128]{2,1,0:T(8,128)S(1)}, u32[]{:S(2)}, u32[]{:S(2)}) collective-permute-start(f32[14,128,128]{2,1,0:T(8,128)S(1)} %collective-permute-done.8.refs_1_), channel_id=1, source_target_pairs={{0,1},{1,0},{2,3},{3,2},{4,5},{5,4},{6,7},{7,6},{8,9},{9,8},{10,11... | collective-permute-start | bytes 2752520 | tf_op jit(solution)/shard_map/ppermute | solution.py:20
  (6 other events, 5.4 us)

commit v2 on v1

--- a/solution.py
+++ b/solution.py
@@ -11,8 +11,8 @@
 KEPT = 48
 A_BLOCKS = 32
 B_BLOCKS = 8
-CHUNKS = (18, 14)
-UNROLL = 4
+CHUNKS = (21, 11)
+UNROLL = 8
 
 
 def from_behind(value, axis, by=1):
@@ -168,8 +168,9 @@
     lists = find_pairs(bounds, tables, slot_table)
     chunk, last, lists, sums = *chunks, lists, sums
     chunk, lists, sums = lax.optimization_barrier((chunk, lists, sums))
-    half = chunk.shape[0] // 2
-    chunk_other = jnp.concatenate([other(chunk[:half]), other(chunk[half:])])
+    third = chunk.shape[0] // 3
+    cuts = (0, third, 2 * third, chunk.shape[0])
+    chunk_other = jnp.concatenate([other(chunk[s:e]) for s, e in zip(cuts, cuts[1:])])
     sums = accumulate(0, lists, (chunk, chunk_other), b_next, sums)
     last, sums = lax.optimization_barrier((last, sums))
     sums = accumulate(1, lists, with_other(last), b_next, sums)

time: 63.1 us -> 62.4 us (0.989)
  waiting for transfers between devices: 26.8 us -> 30.7 us
  starting transfers between devices: 10.5 us -> 7.44 us
  Pallas kernels: 13.2 us -> 11 us
    ppermute x13 -> x14, waiting for transfers between devices: 26.8 us -> 30.7 us  [from_behind(): lax.ppermute(value, axis, [(i, (i + by) % peers) for i in range(peers)])]
    ppermute x13 -> x14, starting transfers between devices: 10.5 us -> 7.44 us  [from_behind(): lax.ppermute(value, axis, [(i, (i + by) % peers) for i in range(peers)])]
    pallas_call x2, Pallas kernels: 5.4 us -> 3.93 us  [find_pairs(): pl.pallas_call(functools.partial(find, bounds, slots), out_shape=jax.Shap...]
    pallas_call x3, Pallas kernels: 7.79 us -> 7.1 us  [accumulate(): pl.pallas_call(body, out_shape=jax.ShapeDtypeStruct((slots, width, width)...]
    unnamed x34 -> x32, local copies, waits for them, and re-layouts: 5.86 us -> 5.95 us
  transfers between devices with their start and end apart: 13 -> 14, of which waited for: 8 -> 9; matrix products, arithmetic and copies ran while one was open for 10% -> 10% of each run, Pallas kernels for 16% -> 13%
where the time goes in v2:
time: 62.4 us; the launch traced here: 61.8 us
  waiting for transfers between devices  30.7 us (49%)
  Pallas kernels  11 us (18%)
  local copies, waits for them, and re-layouts  10.9 us (17%)
  starting transfers between devices  7.44 us (12%)
  other arithmetic  1.52 us (2%)
    ppermute x14, waiting for transfers between devices, from_behind(): lax.ppermute(value, axis, [(i, (i + by) % peers) for i in range(peers)])  30.7 us
    ppermute x14, starting transfers between devices, from_behind(): lax.ppermute(value, axis, [(i, (i + by) % peers) for i in range(peers)])  7.44 us
    pallas_call x3, Pallas kernels, accumulate(): pl.pallas_call(body, out_shape=jax.ShapeDtypeStruct((slots, width, width)...  7.1 us
    unnamed x32, local copies, waits for them, and re-layouts  5.95 us
    pallas_call x2, Pallas kernels, find_pairs(): pl.pallas_call(functools.partial(find, bounds, slots), out_shape=jax.Shap...  3.93 us
    slice x2, local copies, waits for them, and re-layouts, on_device(): pieces = [a_own[s:e] for s, e in zip(bounds, bounds[1:])]  3.49 us
    concatenate x2, other arithmetic, table(): jnp.concatenate([live[step:step + 1], rows, cols, pair_table[step].reshap...  1.43 us
  transfers between devices with their start and end apart: 14, of which 9 were waited for; matrix products, arithmetic and copies ran while one was open for 10% of the time, Pallas kernels for 13%

profile of v2, /device:TPU:0, one launch (start us, length us, event | category | flops | bytes accessed | tf_op | source)
XLA Modules:
  0.0 61.8 jit_solution(15434394532229818675)
XLA Ops:
  0.0 3.1 %collective-permute-start = (s32[32]{0:T(128)}, s32[32]{0:T(128)S(1)}, u32[]{:S(2)}, u32[]{:S(2)}) collective-permute-start(s32[32]{0:T(128)} %bitcast.15), channel_id=1, source_target_pairs={{0,4},{4,8},{8,12},{12,0},{1,5},{5,9},{9,13},{13,1},{2,6},{6,10},{... | collective-permute-start | bytes 392 | tf_op jit(solution)/shard_map/ppermute | solution.py:20
  3.1 2.6 %slice_bitcast_fusion = f32[21,128,128]{2,1,0:T(8,128)} fusion(f32[1,1,1,32,128,128]{5,4,3,2,1,0:T(8,128)} %param.7), kind=kLoop, calls=%fused_computation.1 | loop fusion | bytes 2752512 | tf_op jit(solution)/shard_map/slice | solution.py:145
  5.7 1.1 %collective-permute-done = s32[32]{0:T(128)S(1)} collective-permute-done((s32[32]{0:T(128)}, s32[32]{0:T(128)S(1)}, u32[]{:S(2)}, u32[]{:S(2)}) %collective-permute-start) | collective-permute-done | bytes 160 | tf_op jit(solution)/shard_map/ppermute | solution.py:20
  7.3 3.6 %collective-permute-done.5.refs_2_ = f32[32,128,128]{2,1,0:T(8,128)S(1)} collective-permute-done((f32[32,128,128]{2,1,0:T(8,128)S(1)}, f32[32,128,128]{2,1,0:T(8,128)S(1)}, u32[]{:S(2)}, u32[]{:S(2)}) %collective-permute-start.5) | collective-permute-done | bytes 2097184 | tf_op jit(solution)/shard_map/ppermute | solution.py:20
  11.0 1.4 %copy-done.3 = f32[32,128,128]{2,1,0:T(8,128)} copy-done((f32[32,128,128]{2,1,0:T(8,128)}, f32[32,128,128]{2,1,0:T(8,128)S(1)}, u32[]{:S(2)}) %copy-start.3) | copy-done | bytes 2097176
  12.5 1.7 %collective-permute-start.3 = (f32[8,128,128]{2,1,0:T(8,128)}, f32[8,128,128]{2,1,0:T(8,128)}, u32[]{:S(2)}, u32[]{:S(2)}) collective-permute-start(f32[8,128,128]{2,1,0:T(8,128)} %bitcast.4.refs_3_), channel_id=1, source_target_pairs={{0,2},{2,0},{1,3},{3,1},{4,6},{6,4},{5,7},{7,5},{8,10},{10,8},{9,1... | collective-permute-start | bytes 1572872 | tf_op jit(solution)/shard_map/ppermute | solution.py:20
  14.9 0.7 %pad_add_fusion.own = s32[233]{0:T(256)S(1)} fusion(s32[192]{0:T(256)S(1)} %reshape_squeeze.9, s32[8]{0:T(128)S(1)} %bitcast.17, s32[32]{0:T(128)S(1)} %bitcast.16, s32[1]{0:T(128)} %bitcast.5), kind=kLoop, calls=%fused_computation.3 | loop fusion | flops 699 | bytes 1864 | tf_op jit(solution)/shard_map/concatenate | solution.py:136
  17.3 2.3 %shard_map.73.refs_0_ = s32[4,128]{1,0:T(4,128)} custom-call(s32[233]{0:T(256)} %copy-done.8, s32[233]{0:T(256)} %copy-done.12, s32[64]{0:T(128)} %reshape_squeeze.10.kept), custom_call_target="tpu_custom_call" | custom-call | flops 1 | bytes 1 | tf_op jit(solution)/shard_map/pallas_call | solution.py:75
  19.6 1.6 %copy-done.4 = f32[32,128,128]{2,1,0:T(8,128)S(1)} copy-done((f32[32,128,128]{2,1,0:T(8,128)S(1)}, f32[32,128,128]{2,1,0:T(8,128)}, u32[]{:S(2)}) %copy-start.4) | copy-done | bytes 2097176
  21.2 0.7 %copy-done.6 = s32[4,128]{1,0:T(4,128)S(1)} copy-done((s32[4,128]{1,0:T(4,128)S(1)}, s32[4,128]{1,0:T(4,128)}, u32[]{:S(2)}) %copy-start.6) | copy-done | bytes 2072
  21.9 2.4 %shard_map.74.refs_5_ = f32[24,128,128]{2,1,0:T(8,128)S(1)} custom-call(s32[4,128]{1,0:T(4,128)S(1)} %copy-done.6, f32[32,128,128]{2,1,0:T(8,128)S(1)} %bitcast.14, f32[32,128,128]{2,1,0:T(8,128)S(1)} %copy-done.4, f32[8,128,128]{2,1,0:T(8,128)} %bitcast.4.refs_3_, f32[8,128,128]{2,1,0:T(8,128)} %collective-permute-done.6.refs_4_), custom_call_target="tpu_custom_call" | custom-call | flops 1 | bytes 1 | tf_op jit(solution)/shard_map/pallas_call | solution.py:118
  24.3 1.1 %copy-done.1 = f32[24,128,128]{2,1,0:T(8,128)} copy-done((f32[24,128,128]{2,1,0:T(8,128)}, f32[24,128,128]{2,1,0:T(8,128)S(1)}, u32[]{:S(2)}) %copy-start.1) | copy-done | bytes 1572888
  25.5 1.5 %collective-permute-done.2 = s32[8]{0:T(128)S(1)} collective-permute-done((s32[8]{0:T(128)S(1)}, s32[8]{0:T(128)S(1)}, u32[]{:S(2)}, u32[]{:S(2)}) %collective-permute-start.2) | collective-permute-done | bytes 64 | tf_op jit(solution)/shard_map/ppermute | solution.py:20
  27.0 0.7 %pad_add_fusion.1.own = s32[233]{0:T(256)S(1)} fusion(s32[192]{0:T(256)S(1)} %reshape_squeeze.11, s32[8]{0:T(128)S(1)} %collective-permute-done.2, s32[32]{0:T(128)S(1)} %collective-permute-done, s32[1]{0:T(128)} %bitcast.2), kind=kLoop, calls=%fused_computation.4 | loop fusion | flops 699 | bytes 1864 | tf_op jit(solution)/shard_map/concatenate | solution.py:136
  27.7 0.9 %slice_bitcast_fusion.1 = f32[11,128,128]{2,1,0:T(8,128)} fusion(f32[1,1,1,32,128,128]{5,4,3,2,1,0:T(8,128)S(1)} %copy-done), kind=kLoop, calls=%fused_computation.2 | loop fusion | bytes 1441792 | tf_op jit(solution)/shard_map/slice | solution.py:145
  29.7 1.7 %shard_map.75.refs_0_ = s32[6,128]{1,0:T(8,128)} custom-call(s32[233]{0:T(256)} %copy-done.9, s32[233]{0:T(256)} %copy-done.13, s32[64]{0:T(128)} %reshape_squeeze.10.kept), custom_call_target="tpu_custom_call" | custom-call | flops 1 | bytes 1 | tf_op jit(solution)/shard_map/pallas_call | solution.py:75
  31.4 10.4 %collective-permute-done.1.refs_1_ = f32[21,128,128]{2,1,0:T(8,128)S(1)} collective-permute-done((f32[21,128,128]{2,1,0:T(8,128)}, f32[21,128,128]{2,1,0:T(8,128)S(1)}, u32[]{:S(2)}, u32[]{:S(2)}) %collective-permute-start.1) | collective-permute-done | bytes 1376288 | tf_op jit(solution)/shard_map/ppermute | solution.py:20
  43.0 0.8 %collective-permute-done.10 = f32[7,128,128]{2,1,0:T(8,128)S(1)} collective-permute-done((f32[7,128,128]{2,1,0:T(8,128)S(1)}, f32[7,128,128]{2,1,0:T(8,128)S(1)}, u32[]{:S(2)}, u32[]{:S(2)}) %collective-permute-start.10) | collective-permute-done | bytes 458784 | tf_op jit(solution)/shard_map/ppermute | solution.py:20
  43.8 1.3 %collective-permute-done.11 = f32[7,128,128]{2,1,0:T(8,128)S(1)} collective-permute-done((f32[7,128,128]{2,1,0:T(8,128)S(1)}, f32[7,128,128]{2,1,0:T(8,128)S(1)}, u32[]{:S(2)}, u32[]{:S(2)}) %collective-permute-start.11) | collective-permute-done | bytes 458784 | tf_op jit(solution)/shard_map/ppermute | solution.py:20
  45.1 0.7 %collective-permute-done.9 = f32[7,128,128]{2,1,0:T(8,128)S(1)} collective-permute-done((f32[7,128,128]{2,1,0:T(8,128)S(1)}, f32[7,128,128]{2,1,0:T(8,128)S(1)}, u32[]{:S(2)}, u32[]{:S(2)}) %collective-permute-start.9) | collective-permute-done | bytes 458784 | tf_op jit(solution)/shard_map/ppermute | solution.py:20
  46.0 1.9 %shard_map.76.refs_5_ = f32[24,128,128]{2,1,0:T(8,128)S(1)} custom-call(s32[6,128]{1,0:T(8,128)S(1)} %copy-done.5, f32[21,128,128]{2,1,0:T(8,128)S(1)} %collective-permute-done.1.refs_1_, f32[21,128,128]{2,1,0:T(8,128)S(1)} %pad_maximum_fusion.refs_2_, f32[8,128,128]{2,1,0:T(8,128)} %collective-permute-done.3.refs_3_, ...), custom_call_target="tpu_custom_call" | custom-call | flops 1 | bytes 1 | tf_op jit(solution)/shard_map/pallas_call | solution.py:118
  47.9 9.0 %collective-permute-done.8.refs_1_ = f32[11,128,128]{2,1,0:T(8,128)S(1)} collective-permute-done((f32[11,128,128]{2,1,0:T(8,128)}, f32[11,128,128]{2,1,0:T(8,128)S(1)}, u32[]{:S(2)}, u32[]{:S(2)}) %collective-permute-start.8) | collective-permute-done | bytes 720928 | tf_op jit(solution)/shard_map/ppermute | solution.py:20
  56.9 2.2 %collective-permute-done.13.refs_2_ = f32[11,128,128]{2,1,0:T(8,128)S(1)} collective-permute-done((f32[11,128,128]{2,1,0:T(8,128)S(1)}, f32[11,128,128]{2,1,0:T(8,128)S(1)}, u32[]{:S(2)}, u32[]{:S(2)}) %collective-permute-start.13) | collective-permute-done | bytes 720928 | tf_op jit(solution)/shard_map/ppermute | solution.py:20
  59.0 2.8 %shard_map.77 = f32[24,128,128]{2,1,0:T(8,128)} custom-call(s32[6,128]{1,0:T(8,128)S(1)} %copy-done.5, f32[11,128,128]{2,1,0:T(8,128)S(1)} %collective-permute-done.8.refs_1_, f32[11,128,128]{2,1,0:T(8,128)S(1)} %collective-permute-done.13.refs_2_, f32[8,128,128]{2,1,0:T(8,128)} %collective-permute-done.3.refs_3_, ...), custom_call_target="tpu_custom_call" | custom-call | flops 1 | bytes 1 | tf_op jit(solution)/shard_map/pallas_call | solution.py:118
  (52 shorter events, 5.4 us)
Async XLA Ops:
  0.0 6.8 %copy-start = (f32[1,1,1,32,128,128]{5,4,3,2,1,0:T(8,128)S(1)}, f32[1,1,1,32,128,128]{5,4,3,2,1,0:T(8,128)}, u32[]{:S(2)}) copy-start(f32[1,1,1,32,128,128]{5,4,3,2,1,0:T(8,128)} %param.7) | copy-start | bytes 6291460
  0.0 14.2 %copy-start.10 = (s32[1,1,1,2,2,96]{5,4,3,2,1,0:T(2,128)S(1)}, s32[1,1,1,2,2,96]{5,4,3,2,1,0:T(2,128)}, u32[]{:S(2)}) copy-start(s32[1,1,1,2,2,96]{5,4,3,2,1,0:T(2,128)} %param.11) | copy-start | bytes 4612
  0.0 14.3 %copy-start.11 = (s32[1,1,1,2]{3,2,1,0:T(1,128)S(1)}, s32[1,1,1,2]{3,2,1,0:T(1,128)}, u32[]{:S(2)}) copy-start(s32[1,1,1,2]{3,2,1,0:T(1,128)} %param.12) | copy-start | bytes 28
  0.0 14.9 %copy-start.14 = (s32[1,1,1,32]{3,2,1,0:T(1,128)S(1)}, s32[1,1,1,32]{3,2,1,0:T(1,128)}, u32[]{:S(2)}) copy-start(s32[1,1,1,32]{3,2,1,0:T(1,128)} %param.8) | copy-start | bytes 388
  0.0 14.9 %copy-start.15 = (s32[1,1,1,8]{3,2,1,0:T(1,128)S(1)}, s32[1,1,1,8]{3,2,1,0:T(1,128)}, u32[]{:S(2)}) copy-start(s32[1,1,1,8]{3,2,1,0:T(1,128)} %param.10) | copy-start | bytes 100
  0.0 15.7 %copy-start.7 = (s32[1,1,8,8]{3,2,1,0:T(8,128)S(1)}, s32[1,1,8,8]{3,2,1,0:T(8,128)}, u32[]{:S(2)}) copy-start(s32[1,1,8,8]{3,2,1,0:T(8,128)} %param.13) | copy-start | bytes 772
  0.0 6.8 %collective-permute-start = (s32[32]{0:T(128)}, s32[32]{0:T(128)S(1)}, u32[]{:S(2)}, u32[]{:S(2)}) collective-permute-start(s32[32]{0:T(128)} %bitcast.15), channel_id=1, source_target_pairs={{0,4},{4,8},{8,12},{12,0},{1,5},{5,9},{9,13},{13,1},{2,6},{6,10},{... | collective-permute-start | bytes 392 | tf_op jit(solution)/shard_map/ppermute | solution.py:20
  6.8 4.2 %collective-permute-start.5 = (f32[32,128,128]{2,1,0:T(8,128)S(1)}, f32[32,128,128]{2,1,0:T(8,128)S(1)}, u32[]{:S(2)}, u32[]{:S(2)}) collective-permute-start(f32[32,128,128]{2,1,0:T(8,128)S(1)} %bitcast.13), channel_id=1, source_target_pairs={{0,1},{1,0},{2,3},{3,2},{4,5},{5,4},{6,7},{7,6},{8,9},{9,8},{10,11... | collective-permute-start | bytes 6291464 | tf_op jit(solution)/shard_map/ppermute | solution.py:20
  6.8 35.0 %collective-permute-start.1 = (f32[21,128,128]{2,1,0:T(8,128)}, f32[21,128,128]{2,1,0:T(8,128)S(1)}, u32[]{:S(2)}, u32[]{:S(2)}) collective-permute-start(f32[21,128,128]{2,1,0:T(8,128)} %slice_bitcast_fusion), channel_id=1, source_target_pairs={{0,4},{4,8},{8,12},{12,0},{1,5},{5,9},{9,13},{13,1},{2,6},{6,10},{... | collective-permute-start | bytes 4128776 | tf_op jit(solution)/shard_map/ppermute | solution.py:20
  12.3 7.3 %collective-permute-start.6 = (f32[8,128,128]{2,1,0:T(8,128)}, f32[8,128,128]{2,1,0:T(8,128)}, u32[]{:S(2)}, u32[]{:S(2)}) collective-permute-start(f32[8,128,128]{2,1,0:T(8,128)} %bitcast.4.refs_3_), channel_id=1, source_target_pairs={{0,1},{1,0},{2,3},{3,2},{4,5},{5,4},{6,7},{7,6},{8,9},{9,8},{10,11... | collective-permute-start | bytes 1572872 | tf_op jit(solution)/shard_map/ppermute | solution.py:20
  12.5 14.5 %collective-permute-start.3 = (f32[8,128,128]{2,1,0:T(8,128)}, f32[8,128,128]{2,1,0:T(8,128)}, u32[]{:S(2)}, u32[]{:S(2)}) collective-permute-start(f32[8,128,128]{2,1,0:T(8,128)} %bitcast.4.refs_3_), channel_id=1, source_target_pairs={{0,2},{2,0},{1,3},{3,1},{4,6},{6,4},{5,7},{7,5},{8,10},{10,8},{9,1... | collective-permute-start | bytes 1572872 | tf_op jit(solution)/shard_map/ppermute | solution.py:20
  15.6 1.2 %collective-permute-start.4 = (s32[233]{0:T(256)S(1)}, s32[233]{0:T(256)S(1)}, u32[]{:S(2)}, u32[]{:S(2)}) collective-permute-start(s32[233]{0:T(256)S(1)} %pad_add_fusion.own), channel_id=1, source_target_pairs={{0,1},{1,0},{2,3},{3,2},{4,5},{5,4},{6,7},{7,6},{8,9},{9,8},{10,11... | collective-permute-start | bytes 2804 | tf_op jit(solution)/shard_map/ppermute | solution.py:20
  16.4 10.6 %collective-permute-start.2 = (s32[8]{0:T(128)S(1)}, s32[8]{0:T(128)S(1)}, u32[]{:S(2)}, u32[]{:S(2)}) collective-permute-start(s32[8]{0:T(128)S(1)} %bitcast.18), channel_id=1, source_target_pairs={{0,2},{2,0},{1,3},{3,1},{4,6},{6,4},{5,7},{7,5},{8,10},{10,8},{9,1... | collective-permute-start | bytes 104 | tf_op jit(solution)/shard_map/ppermute | solution.py:20
  19.6 1.6 %copy-start.4 = (f32[32,128,128]{2,1,0:T(8,128)S(1)}, f32[32,128,128]{2,1,0:T(8,128)}, u32[]{:S(2)}) copy-start(f32[32,128,128]{2,1,0:T(8,128)} %copy-done.3) | copy-start | bytes 6291460
  27.7 1.4 %copy-start.9 = (s32[233]{0:T(256)}, s32[233]{0:T(256)S(1)}, u32[]{:S(2)}) copy-start(s32[233]{0:T(256)S(1)} %pad_add_fusion.1.own) | copy-start | bytes 2800
  27.7 1.4 %collective-permute-start.7 = (s32[233]{0:T(256)S(1)}, s32[233]{0:T(256)S(1)}, u32[]{:S(2)}, u32[]{:S(2)}) collective-permute-start(s32[233]{0:T(256)S(1)} %pad_add_fusion.1.own), channel_id=1, source_target_pairs={{0,1},{1,0},{2,3},{3,2},{4,5},{5,4},{6,7},{7,6},{8,9},{9,8},{10,11... | collective-permute-start | bytes 2804 | tf_op jit(solution)/shard_map/ppermute | solution.py:20
  28.7 28.2 %collective-permute-start.8 = (f32[11,128,128]{2,1,0:T(8,128)}, f32[11,128,128]{2,1,0:T(8,128)S(1)}, u32[]{:S(2)}, u32[]{:S(2)}) collective-permute-start(f32[11,128,128]{2,1,0:T(8,128)} %slice_bitcast_fusion.1), channel_id=1, source_target_pairs={{0,4},{4,8},{8,12},{12,0},{1,5},{5,9},{9,13},{13,1},{2,6},{6,10},{... | collective-permute-start | bytes 2162696 | tf_op jit(solution)/shard_map/ppermute | solution.py:20
  41.9 1.9 %collective-permute-start.10 = (f32[7,128,128]{2,1,0:T(8,128)S(1)}, f32[7,128,128]{2,1,0:T(8,128)S(1)}, u32[]{:S(2)}, u32[]{:S(2)}) collective-permute-start(f32[7,128,128]{2,1,0:T(8,128)S(1)} %get-tuple-element.37), channel_id=1, source_target_pairs={{0,1},{1,0},{2,3},{3,2},{4,5},{5,4},{6,7},{7,6},{8,9},{9,8},{10,11... | collective-permute-start | bytes 1376264 | tf_op jit(solution)/shard_map/ppermute | solution.py:20
  42.0 3.1 %collective-permute-start.11 = (f32[7,128,128]{2,1,0:T(8,128)S(1)}, f32[7,128,128]{2,1,0:T(8,128)S(1)}, u32[]{:S(2)}, u32[]{:S(2)}) collective-permute-start(f32[7,128,128]{2,1,0:T(8,128)S(1)} %get-tuple-element.36), channel_id=1, source_target_pairs={{0,1},{1,0},{2,3},{3,2},{4,5},{5,4},{6,7},{7,6},{8,9},{9,8},{10,11... | collective-permute-start | bytes 1376264 | tf_op jit(solution)/shard_map/ppermute | solution.py:20
  42.5 3.5 %copy-start.2 = (f32[24,128,128]{2,1,0:T(8,128)S(1)}, f32[24,128,128]{2,1,0:T(8,128)}, u32[]{:S(2)}) copy-start(f32[24,128,128]{2,1,0:T(8,128)} %copy-done.1) | copy-start | bytes 4718596
  42.5 3.5 %copy-start.5 = (s32[6,128]{1,0:T(8,128)S(1)}, s32[6,128]{1,0:T(8,128)}, u32[]{:S(2)}) copy-start(s32[6,128]{1,0:T(8,128)} %shard_map.75.refs_0_) | copy-start | bytes 9220
  42.5 3.4 %collective-permute-start.9 = (f32[7,128,128]{2,1,0:T(8,128)S(1)}, f32[7,128,128]{2,1,0:T(8,128)S(1)}, u32[]{:S(2)}, u32[]{:S(2)}) collective-permute-start(f32[7,128,128]{2,1,0:T(8,128)S(1)} %get-tuple-element.35), channel_id=1, source_target_pairs={{0,1},{1,0},{2,3},{3,2},{4,5},{5,4},{6,7},{7,6},{8,9},{9,8},{10,11... | collective-permute-start | bytes 1376264 | tf_op jit(solution)/shard_map/ppermute | solution.py:20
  42.5 3.4 %collective-permute-start.12 = (f32[8,128,128]{2,1,0:T(8,128)}, f32[8,128,128]{2,1,0:T(8,128)S(1)}, u32[]{:S(2)}, u32[]{:S(2)}) collective-permute-start(f32[8,128,128]{2,1,0:T(8,128)} %collective-permute-done.3.refs_3_), channel_id=1, source_target_pairs={{0,1},{1,0},{2,3},{3,2},{4,5},{5,4},{6,7},{7,6},{8,9},{9,8},{10,11... | collective-permute-start | bytes 1572872 | tf_op jit(solution)/shard_map/ppermute | solution.py:20
  56.9 2.2 %collective-permute-start.13 = (f32[11,128,128]{2,1,0:T(8,128)S(1)}, f32[11,128,128]{2,1,0:T(8,128)S(1)}, u32[]{:S(2)}, u32[]{:S(2)}) collective-permute-start(f32[11,128,128]{2,1,0:T(8,128)S(1)} %collective-permute-done.8.refs_1_), channel_id=1, source_target_pairs={{0,1},{1,0},{2,3},{3,2},{4,5},{5,4},{6,7},{7,6},{8,9},{9,8},{10,11... | collective-permute-start | bytes 2162696 | tf_op jit(solution)/shard_map/ppermute | solution.py:20
  (6 other events, 5.5 us)
